TPU v7x, 32 devices: a whole 2x2x4 slice. The times are simulated.
32 devices in a mesh: gx: 4 (over z), gy: 2 (over y), gz: 4 (over x, core).
Axes of the slice: x: 2, y: 2, z: 4, core: 2. Of those that a mesh axis runs over, the one named last changes fastest.
Arguments:
- populations: float32 [19, 16, 32, 1024], P(None, None, ('gy', 'gz'), 'gx'), may hold values from 0 to 0.5, as said below
- cell_type: int32 [16, 32, 1024], P(None, ('gy', 'gz'), 'gx'), may hold values from 0 to 2, as said below
- adjoint: float32 [7, 16, 32, 1024], P(None, 'gz', 'gy', 'gx'), may hold values from -6 to 6
Outputs:
- flow_next: float32 [19, 16, 32, 1024], P(None, None, ('gy', 'gz'), 'gx')
- adjoint_prev: float32 [7, 16, 32, 1024], P(None, 'gz', 'gy', 'gx')
Inputs may be any that keep to these rules, and one draw needn't show every extreme that they name: `cell_type`: layers below 8 are solid (code 1), with code 2 cells only in layer 0; layers from 8 on hold codes 0 and 1, and a cell's code is the same in all of them. `populations`: each population is its lattice weight times a positive factor near one.
All inputs are finite; a program needn't handle non-finite values.
Results may differ from a plain program's by a relative error of at most 0.000065.
Values sent between devices are 32-bit elements; how exact they have to be, the bound alone decides.
A program may use at most 64 MiB of HBM per device.

v0:
```python
import jax
import jax.numpy as jnp
from jax import lax
from jax.sharding import PartitionSpec as P

VEL19 = [
    (0, 0, 0),
    (1, 0, 0),
    (-1, 0, 0),
    (0, 1, 0),
    (0, -1, 0),
    (0, 0, 1),
    (0, 0, -1),
    (1, 1, 0),
    (-1, -1, 0),
    (1, -1, 0),
    (-1, 1, 0),
    (1, 0, 1),
    (-1, 0, -1),
    (1, 0, -1),
    (-1, 0, 1),
    (0, 1, 1),
    (0, -1, -1),
    (0, 1, -1),
    (0, -1, 1),
]
WEIGHT19 = [1.0 / 3.0] + [1.0 / 18.0] * 6 + [1.0 / 36.0] * 12
OPPOSITE = [0, 2, 1, 4, 3, 6, 5, 8, 7, 10, 9, 12, 11, 14, 13, 16, 15, 18, 17]
VEL7 = [(0, 0, 0), (1, 0, 0), (-1, 0, 0), (0, 1, 0), (0, -1, 0), (0, 0, 1), (0, 0, -1)]
WEIGHT7 = [0.25] + [0.125] * 6
OMEGA_FLOW = 1.6
OMEGA_FLUID = 1.25
OMEGA_SOLID = 1.6


def padded_2(value, sides, width):
    for axis, dim in sides:
        devices, length = (lax.axis_size(axis), value.shape[dim])
        up = [(i, (i + 1) % devices) for i in range(devices - 1)]
        down = [(j, i) for i, j in up]
        last = lax.slice_in_dim(value, length - width, length, axis=dim)
        leading = lax.slice_in_dim(value, 0, width, axis=dim)
        before = lax.ppermute(last, axis, up)
        after = lax.ppermute(leading, axis, down)
        value = jnp.concatenate([before, value, after], axis=dim)
    return value


def collide(pops):
    table = jnp.array(VEL19, jnp.float32).T
    density = jnp.sum(pops, axis=0)
    velocity = jnp.tensordot(table, pops, axes=1, precision=lax.Precision.HIGHEST) / density
    usq = jnp.sum(velocity * velocity, axis=0)
    outs = []
    for i in range(19):
        cx, cy, cz = VEL19[i]
        cu = cx * velocity[0] + cy * velocity[1] + cz * velocity[2]
        feq = WEIGHT19[i] * density * (1.0 + 3.0 * cu + 4.5 * cu * cu - 1.5 * usq)
        outs.append(pops[i] - OMEGA_FLOW * (pops[i] - feq))
    return jnp.stack(outs)


def stream(padded, post, pops, fluid):
    depth, rows, cols = fluid.shape
    outs = []
    for i in range(19):
        cx, cy, cz = VEL19[i]
        src = padded[i, 1 - cz : 1 - cz + depth, 1 - cy : 1 - cy + rows, 1 - cx : 1 - cx + cols]
        flag = padded[19, 1 - cz : 1 - cz + depth, 1 - cy : 1 - cy + rows, 1 - cx : 1 - cx + cols]
        pulled = flag * src + (1.0 - flag) * post[OPPOSITE[i]]
        outs.append(jnp.where(fluid > 0.5, pulled, pops[i]))
    return jnp.stack(outs)


def thermal(padded, velocity, codes):
    depth, rows, cols = codes.shape
    pulled = []
    for j in range(7):
        ex, ey, ez = VEL7[j]
        pulled.append(
            padded[j, 1 + ez : 1 + ez + depth, 1 + ey : 1 + ey + rows, 1 + ex : 1 + ex + cols]
        )
    mean_term = sum((WEIGHT7[j] * pulled[j] for j in range(7)))
    flux = [sum((WEIGHT7[j] * VEL7[j][k] * pulled[j] for j in range(7))) for k in range(3)]
    coupled = mean_term + 4.0 * (
        velocity[0] * flux[0] + velocity[1] * flux[1] + velocity[2] * flux[2]
    )
    omega = jnp.where(codes == 0.0, OMEGA_FLUID, OMEGA_SOLID)
    source = jnp.where(codes == 2.0, 1.0, 0.0)
    return jnp.stack([(1.0 - omega) * pulled[j] + omega * coupled + source for j in range(7)])


def per_device(populations, cell_type, adjoint):
    fluid = jnp.where(cell_type == 0, 1.0, 0.0).astype(jnp.float32)
    post = collide(populations)
    stacked = jnp.concatenate([post, fluid[None]], axis=0)
    framed = padded_2(stacked, (("gx", 3), (("gy", "gz"), 2)), 1)
    padded = jnp.pad(framed, ((0, 0), (1, 1), (0, 0), (0, 0)))
    flow_next = stream(padded, post, populations, fluid)
    density = jnp.sum(flow_next, axis=0)
    table = jnp.array(VEL19, jnp.float32).T
    velocity = (
        jnp.tensordot(table, flow_next, axes=1, precision=lax.Precision.HIGHEST) / density * fluid
    )
    carried = jnp.concatenate([velocity, cell_type.astype(jnp.float32)[None]], axis=0)
    heat_pad = padded_2(adjoint, (("gx", 3), ("gy", 2), ("gz", 1)), 1)
    regrouped = lax.all_to_all(carried, "gz", split_axis=1, concat_axis=2, tiled=True)
    adjoint_prev = thermal(heat_pad, regrouped[:3], regrouped[3])
    return (flow_next, adjoint_prev)


def solution(mesh):
    placed = (
        P(None, None, ("gy", "gz"), "gx"),
        P(None, ("gy", "gz"), "gx"),
        P(None, "gz", "gy", "gx"),
    )
    return jax.shard_map(
        per_device,
        mesh=mesh,
        in_specs=placed,
        out_specs=(P(None, None, ("gy", "gz"), "gx"), P(None, "gz", "gy", "gx")),
        check_vma=False,
    )
```

profile of v0, /device:TPU:14, one launch (start us, length us, event | category | flops | bytes accessed | tf_op | source)
XLA Modules:
  0.0 67.1 jit_solution(31192328688657349)
XLA Ops:
  0.6 1.6 %fusion.363 = (f32[1,16,4,256]{3,2,1,0:T(4,128)S(1)}, f32[1,16,4,256]{3,2,1,0:T(4,128)S(1)}, f32[1,16,4,256]{3,2,1,0:T(4,128)S(1)}, f32[1,16,4,256]{3,2,1,0:T(4,...) fusion(f32[19,16,4,256]{3,2,1,0:T(4,128)} %param.5), kind=kLoop, calls=%fused_computation.524 | loop fusion | bytes 2490368 | tf_op jit(solution)/shard_map/slice | solution.py:59
  2.8 0.5 copy-done.42
  3.3 1.6 %fusion.3 = f32[3,16,4,256]{3,0,2,1:T(4,128)S(1)} fusion(f32[19,3,1,1]{0,1,3,2:T(4,128)S(1)} %copy-done.42, f32[19,16,4,256]{3,2,1,0:T(4,128)S(1)} %copy-done), kind=kOutput, calls=%fused_computation.9 | convolution fusion | flops 11206656 | bytes 1442020 | tf_op jit(solution)/shard_map/dot_general | solution.py:52
  4.9 0.6 broadcast_select_fusion
  7.3 0.5 copy.224
  7.8 3.5 %collective-permute-start = (f32[20,16,4,1]{0,1,3,2:T(8,128)S(1)}, f32[20,16,4,1]{0,1,3,2:T(8,128)S(1)}, u32[]{:S(2)}, u32[]{:S(2)}) collective-permute-start(f32[20,16,4,1]{0,1,3,2:T(8,128)S(1)} %copy.224), channel_id=1, source_target_pairs={{0,8},{8,16},{16,24},{1,9},{9,17},{17,25},{2,10},{10,18},{18,26},{... | collective-permute-start | bytes 15368 | tf_op jit(solution)/shard_map/ppermute | solution.py:43
  11.3 0.5 copy.226
  11.8 2.4 %collective-permute-start.1 = (f32[20,16,4,1]{0,1,3,2:T(8,128)S(1)}, f32[20,16,4,1]{0,1,3,2:T(8,128)S(1)}, u32[]{:S(2)}, u32[]{:S(2)}) collective-permute-start(f32[20,16,4,1]{0,1,3,2:T(8,128)S(1)} %copy.226), channel_id=1, source_target_pairs={{8,0},{16,8},{24,16},{9,1},{17,9},{25,17},{10,2},{18,10},{26,18},{... | collective-permute-start | bytes 15368 | tf_op jit(solution)/shard_map/ppermute | solution.py:44
  14.2 0.7 %copy.225 = f32[20,16,4,1]{3,1,2,0:T(8,128)S(1)} copy(f32[20,16,4,1]{0,1,3,2:T(8,128)S(1)} %collective-permute-done) | data formatting | bytes 10240 | tf_op jit(solution)/shard_map/ppermute | solution.py:43
  15.0 2.7 %collective-permute-done.1 = f32[20,16,4,1]{0,1,3,2:T(8,128)S(1)} collective-permute-done((f32[20,16,4,1]{0,1,3,2:T(8,128)S(1)}, f32[20,16,4,1]{0,1,3,2:T(8,128)S(1)}, u32[]{:S(2)}, u32[]{:S(2)}) %collective-permute-start.1) | collective-permute-done | bytes 5152 | tf_op jit(solution)/shard_map/ppermute | solution.py:44
  17.6 0.7 %copy.227 = f32[20,16,4,1]{3,1,2,0:T(8,128)S(1)} copy(f32[20,16,4,1]{0,1,3,2:T(8,128)S(1)} %collective-permute-done.1) | data formatting | bytes 10240 | tf_op jit(solution)/shard_map/ppermute | solution.py:44
  18.8 1.9 %collective-permute-start.2 = (f32[20,16,1,258]{3,1,2,0:T(8,128)S(1)}, f32[20,16,1,258]{3,1,2,0:T(8,128)S(1)}, u32[]{:S(2)}, u32[]{:S(2)}) collective-permute-start(f32[20,16,1,258]{3,1,2,0:T(8,128)S(1)} %get-tuple-element.40), channel_id=1, source_target_pairs={{0,1},{1,2},{2,3},{3,4},{4,5},{5,6},{6,7},{8,9},{9,10},{10,11},{11... | collective-permute-start | bytes 990728 | tf_op jit(solution)/shard_map/ppermute | solution.py:43
  20.8 3.6 %collective-permute-start.3 = (f32[20,16,1,258]{3,1,2,0:T(8,128)S(1)}, f32[20,16,1,258]{3,1,2,0:T(8,128)S(1)}, u32[]{:S(2)}, u32[]{:S(2)}) collective-permute-start(f32[20,16,1,258]{3,1,2,0:T(8,128)S(1)} %get-tuple-element.41), channel_id=1, source_target_pairs={{1,0},{2,1},{3,2},{4,3},{5,4},{6,5},{7,6},{9,8},{10,9},{11,10},{12... | collective-permute-start | bytes 990728 | tf_op jit(solution)/shard_map/ppermute | solution.py:44
  24.4 0.8 %fusion.364 = (f32[7,4,16,1]{3,2,1,0:T(8,128)}, f32[7,4,16,1]{3,2,1,0:T(8,128)}) fusion(f32[7,4,16,256]{3,2,1,0:T(8,128)S(1)} %copy-done.1), kind=kLoop, calls=%fused_computation.525 | loop fusion | bytes 7168 | tf_op jit(solution)/shard_map/slice | solution.py:41
  25.2 2.3 %collective-permute-start.4 = (f32[7,4,16,1]{3,2,1,0:T(8,128)}, f32[7,4,16,1]{3,2,1,0:T(8,128)}, u32[]{:S(2)}, u32[]{:S(2)}) collective-permute-start(f32[7,4,16,1]{3,2,1,0:T(8,128)} %get-tuple-element.68), channel_id=1, source_target_pairs={{8,0},{16,8},{24,16},{9,1},{17,9},{25,17},{10,2},{18,10},{26,18},{... | collective-permute-start | bytes 5384 | tf_op jit(solution)/shard_map/ppermute | solution.py:44
  27.6 3.5 %collective-permute-start.5 = (f32[7,4,16,1]{3,2,1,0:T(8,128)}, f32[7,4,16,1]{3,2,1,0:T(8,128)}, u32[]{:S(2)}, u32[]{:S(2)}) collective-permute-start(f32[7,4,16,1]{3,2,1,0:T(8,128)} %get-tuple-element.67), channel_id=1, source_target_pairs={{0,8},{8,16},{16,24},{1,9},{9,17},{17,25},{2,10},{10,18},{18,26},{... | collective-permute-start | bytes 5384 | tf_op jit(solution)/shard_map/ppermute | solution.py:43
  31.4 1.7 %select_maximum_fusion = f32[20,18,6,258]{3,1,2,0:T(8,128)S(1)} fusion(f32[20,16,1,258]{3,1,2,0:T(8,128)S(1)} %collective-permute-done.3, f32[20,16,1,258]{3,1,2,0:T(8,128)S(1)} %collective-permute-done.2, f32[20,16,4,1]{3,1,2,0:T(8,128)S(1)} %copy.227, f32[20,16,4,256]{3,1,2,0:T(8,128)S(1)} %constant_dynamic-update-slice_fusion, f32[20,16,4,1]{3,1,2,0:T(8,128)S(1)} %copy.225), kind=kLoop, calls=%fused_computation.2 | loop fusion | flops 6687360 | bytes 4210560 | tf_op jit(solution)/shard_map/concatenate | solution.py:45
  33.4 1.2 %add_add_fusion = (f32[16,4,256]{2,0,1:T(8,128)S(1)}, f32[16,4,256]{2,0,1:T(8,128)S(1)}, f32[16,4,256]{2,0,1:T(8,128)S(1)}, f32[16,4,256]{2,0,1:T(8,128)S(1)}, f...) fusion(f32[1,16,4,256]{3,2,1,0:T(4,128)S(1)} %copy-done.31, ...), kind=kLoop, calls=%fused_computation.507 | loop fusion | flops 6471680 | bytes 6257664 | tf_op jit(solution)/shard_map/reduce_sum | solution.py:100
  35.3 2.0 %fusion.11 = f32[3,16,4,256]{3,0,2,1:T(4,128)S(1)} fusion(f32[19,3,1,1]{0,1,3,2:T(4,128)S(1)} %copy-done.43, f32[19,16,4,256]{3,1,2,0:T(8,128)S(1)} %constant_dynamic-update-slice_fusion.20, f32[16,4,256]{2,1,0:T(4,128)S(1)} %copy.232, f32[16,4,256]{2,1,0:T(4,128)S(1)} %copy.231), kind=kOutput, calls=%fused_computation.13 | convolution fusion | flops 11304960 | bytes 1573092 | tf_op jit(solution)/shard_map/dot_general | solution.py:103
  37.3 0.8 %pad_maximum_fusion.3 = f32[4,16,4,256]{3,0,2,1:T(4,128)} fusion(f32[1,16,4,256]{3,0,2,1:T(1,128)S(1)} %broadcast_in_dim.36, f32[3,16,4,256]{3,0,2,1:T(4,128)S(1)} %fusion.11), kind=kLoop, calls=%fused_computation.17 | loop fusion | flops 65536 | bytes 524288 | tf_op jit(solution)/shard_map/concatenate | solution.py:105
  38.1 5.7 %all-to-all-start = ((f32[4,16,4,256]{3,0,2,1:T(4,128)}), f32[4,16,4,256]{3,0,2,1:T(4,128)S(1)}, u32[]{:S(2)}, u32[]{:S(2)}) async-start(f32[4,16,4,256]{3,0,2,1:T(4,128)} %pad_maximum_fusion.3), calls=%async_computation | async-start | bytes 524288 | tf_op jit(solution)/shard_map/all_to_all | solution.py:107
  43.8 1.4 %pad_maximum_fusion.43 = (f32[7,4,1,258]{3,2,1,0:T(1,128)S(1)}, f32[7,4,1,258]{3,2,1,0:T(1,128)S(1)}) fusion(f32[7,4,16,1]{3,2,1,0:T(8,128)} %collective-permute-done.4, f32[7,4,16,256]{3,2,1,0:T(8,128)S(1)} %copy-done.1, f32[7,4,16,1]{3,2,1,0:T(8,128)} %collective-permute-done.5), kind=kLoop, calls=%fused_computation.516 | loop fusion | flops 28896 | bytes 520128 | tf_op jit(solution)/shard_map/concatenate | solution.py:45
  45.2 3.2 %collective-permute-start.6 = (f32[7,4,1,258]{3,2,1,0:T(1,128)S(1)}, f32[7,4,1,258]{3,2,1,0:T(1,128)S(1)}, u32[]{:S(2)}, u32[]{:S(2)}) collective-permute-start(f32[7,4,1,258]{3,2,1,0:T(1,128)S(1)} %get-tuple-element.66), channel_id=1, source_target_pairs={{4,0},{5,1},{6,2},{7,3},{12,8},{13,9},{14,10},{15,11},{20,16},{21,... | collective-permute-start | bytes 86696 | tf_op jit(solution)/shard_map/ppermute | solution.py:44
  48.4 1.3 %collective-permute-start.7 = (f32[7,4,1,258]{3,2,1,0:T(1,128)S(1)}, f32[7,4,1,258]{3,2,1,0:T(1,128)S(1)}, u32[]{:S(2)}, u32[]{:S(2)}) collective-permute-start(f32[7,4,1,258]{3,2,1,0:T(1,128)S(1)} %get-tuple-element.65), channel_id=1, source_target_pairs={{0,4},{1,5},{2,6},{3,7},{8,12},{9,13},{10,14},{11,15},{16,20},{17,... | collective-permute-start | bytes 86696 | tf_op jit(solution)/shard_map/ppermute | solution.py:43
  50.1 4.2 %collective-permute-done.7 = f32[7,4,1,258]{3,2,1,0:T(1,128)S(1)} collective-permute-done((f32[7,4,1,258]{3,2,1,0:T(1,128)S(1)}, f32[7,4,1,258]{3,2,1,0:T(1,128)S(1)}, u32[]{:S(2)}, u32[]{:S(2)}) %collective-permute-start.7) | collective-permute-done | bytes 28928 | tf_op jit(solution)/shard_map/ppermute | solution.py:43
  54.3 1.2 %pad_maximum_fusion.4 = (f32[7,1,18,258]{3,2,1,0:T(8,128)S(1)}, f32[7,1,18,258]{3,2,1,0:T(8,128)S(1)}) fusion(f32[7,4,1,258]{3,2,1,0:T(1,128)S(1)} %collective-permute-done.6, f32[7,4,1,258]{3,2,1,0:T(1,128)S(1)} %collective-permute-done.7, f32[7,4,16,1]{3,2,1,0:T(8,128)} %collective-permute-done.4, f32[7,4,16,256]{3,2,1,0:T(8,128)S(1)} %copy-done.1, ...), kind=kLoop, calls=%fused_computation.20 | loop fusion | flops 260064 | bytes 780192 | tf_op jit(solution)/shard_map/concatenate | solution.py:45
  55.5 2.1 %collective-permute-start.8 = (f32[7,1,18,258]{3,2,1,0:T(8,128)S(1)}, f32[7,1,18,258]{3,2,1,0:T(8,128)S(1)}, u32[]{:S(2)}, u32[]{:S(2)}) collective-permute-start(f32[7,1,18,258]{3,2,1,0:T(8,128)S(1)} %get-tuple-element.64), channel_id=1, source_target_pairs={{1,0},{2,1},{3,2},{5,4},{6,5},{7,6},{9,8},{10,9},{11,10},{13,12},{... | collective-permute-start | bytes 390104 | tf_op jit(solution)/shard_map/ppermute | solution.py:44
  57.5 2.3 %collective-permute-start.9 = (f32[7,1,18,258]{3,2,1,0:T(8,128)S(1)}, f32[7,1,18,258]{3,2,1,0:T(8,128)S(1)}, u32[]{:S(2)}, u32[]{:S(2)}) collective-permute-start(f32[7,1,18,258]{3,2,1,0:T(8,128)S(1)} %get-tuple-element.63), channel_id=1, source_target_pairs={{0,1},{1,2},{2,3},{4,5},{5,6},{6,7},{8,9},{9,10},{10,11},{12,13},{... | collective-permute-start | bytes 390104 | tf_op jit(solution)/shard_map/ppermute | solution.py:43
  59.8 1.9 %copy.238 = f32[19,16,4,256]{3,2,1,0:T(4,128)} copy(f32[19,16,4,256]{3,1,2,0:T(8,128)S(1)} %constant_dynamic-update-slice_fusion.20) | data formatting | bytes 2490368
  62.4 2.8 %collective-permute-done.9 = f32[7,1,18,258]{3,2,1,0:T(8,128)S(1)} collective-permute-done((f32[7,1,18,258]{3,2,1,0:T(8,128)S(1)}, f32[7,1,18,258]{3,2,1,0:T(8,128)S(1)}, u32[]{:S(2)}, u32[]{:S(2)}) %collective-permute-start.9) | collective-permute-done | bytes 130064 | tf_op jit(solution)/shard_map/ppermute | solution.py:43
  65.2 1.0 %constant_dynamic-update-slice_fusion.45 = (f32[7,4,16,256]{3,2,1,0:T(8,128)S(1)}, f32[1,4,16,256]{3,2,1,0:T(8,128)S(1)}, f32[1,4,16,256]{3,2,1,0:T(8,128)S(1)},...) fusion(f32[1,4,16,256]{3,2,1,0:T(8,128)S(1)} %select_n.127, ...), kind=kLoop, calls=%fused_computation.110 | loop fusion | flops 1130495 | bytes 1981952
  66.4 0.8 %copy-done.41 = f32[7,4,16,256]{3,2,1,0:T(8,128)} copy-done((f32[7,4,16,256]{3,2,1,0:T(8,128)}, f32[7,4,16,256]{3,2,1,0:T(8,128)S(1)}, u32[]{:S(2)}) %copy-start.41) | copy-done | bytes 458776
  (159 shorter events, 4.0 us)
Async XLA Ops:
  2.4 3.3 %copy-start.36 = (f32[1,16,4,256]{3,2,1,0:T(4,128)}, f32[1,16,4,256]{3,2,1,0:T(4,128)S(1)}, u32[]{:S(2)}) copy-start(f32[1,16,4,256]{3,2,1,0:T(4,128)S(1)} %get-tuple-element.61) | copy-start | bytes 196612
  2.4 3.3 %copy-start.28 = (f32[1,16,4,256]{3,2,1,0:T(4,128)}, f32[1,16,4,256]{3,2,1,0:T(4,128)S(1)}, u32[]{:S(2)}) copy-start(f32[1,16,4,256]{3,2,1,0:T(4,128)S(1)} %get-tuple-element.60) | copy-start | bytes 196612
  2.4 3.4 %copy-start.26 = (f32[1,16,4,256]{3,2,1,0:T(4,128)}, f32[1,16,4,256]{3,2,1,0:T(4,128)S(1)}, u32[]{:S(2)}) copy-start(f32[1,16,4,256]{3,2,1,0:T(4,128)S(1)} %get-tuple-element.59) | copy-start | bytes 196612
  2.4 3.5 %copy-start.24 = (f32[1,16,4,256]{3,2,1,0:T(4,128)}, f32[1,16,4,256]{3,2,1,0:T(4,128)S(1)}, u32[]{:S(2)}) copy-start(f32[1,16,4,256]{3,2,1,0:T(4,128)S(1)} %get-tuple-element.58) | copy-start | bytes 196612
  2.4 3.6 %copy-start.22 = (f32[1,16,4,256]{3,2,1,0:T(4,128)}, f32[1,16,4,256]{3,2,1,0:T(4,128)S(1)}, u32[]{:S(2)}) copy-start(f32[1,16,4,256]{3,2,1,0:T(4,128)S(1)} %get-tuple-element.57) | copy-start | bytes 196612
  2.4 3.6 %copy-start.34 = (f32[1,16,4,256]{3,2,1,0:T(4,128)}, f32[1,16,4,256]{3,2,1,0:T(4,128)S(1)}, u32[]{:S(2)}) copy-start(f32[1,16,4,256]{3,2,1,0:T(4,128)S(1)} %get-tuple-element.56) | copy-start | bytes 196612
  2.4 3.7 %copy-start.32 = (f32[1,16,4,256]{3,2,1,0:T(4,128)}, f32[1,16,4,256]{3,2,1,0:T(4,128)S(1)}, u32[]{:S(2)}) copy-start(f32[1,16,4,256]{3,2,1,0:T(4,128)S(1)} %get-tuple-element.55) | copy-start | bytes 196612
  2.4 3.7 %copy-start.20 = (f32[1,16,4,256]{3,2,1,0:T(4,128)}, f32[1,16,4,256]{3,2,1,0:T(4,128)S(1)}, u32[]{:S(2)}) copy-start(f32[1,16,4,256]{3,2,1,0:T(4,128)S(1)} %get-tuple-element.54) | copy-start | bytes 196612
  2.4 3.8 %copy-start.18 = (f32[1,16,4,256]{3,2,1,0:T(4,128)}, f32[1,16,4,256]{3,2,1,0:T(4,128)S(1)}, u32[]{:S(2)}) copy-start(f32[1,16,4,256]{3,2,1,0:T(4,128)S(1)} %get-tuple-element.53) | copy-start | bytes 196612
  2.4 3.9 %copy-start.16 = (f32[1,16,4,256]{3,2,1,0:T(4,128)}, f32[1,16,4,256]{3,2,1,0:T(4,128)S(1)}, u32[]{:S(2)}) copy-start(f32[1,16,4,256]{3,2,1,0:T(4,128)S(1)} %get-tuple-element.52) | copy-start | bytes 196612
  2.5 3.9 %copy-start.14 = (f32[1,16,4,256]{3,2,1,0:T(4,128)}, f32[1,16,4,256]{3,2,1,0:T(4,128)S(1)}, u32[]{:S(2)}) copy-start(f32[1,16,4,256]{3,2,1,0:T(4,128)S(1)} %get-tuple-element.51) | copy-start | bytes 196612
  2.5 4.0 %copy-start.12 = (f32[1,16,4,256]{3,2,1,0:T(4,128)}, f32[1,16,4,256]{3,2,1,0:T(4,128)S(1)}, u32[]{:S(2)}) copy-start(f32[1,16,4,256]{3,2,1,0:T(4,128)S(1)} %get-tuple-element.50) | copy-start | bytes 196612
  2.5 4.0 %copy-start.10 = (f32[1,16,4,256]{3,2,1,0:T(4,128)}, f32[1,16,4,256]{3,2,1,0:T(4,128)S(1)}, u32[]{:S(2)}) copy-start(f32[1,16,4,256]{3,2,1,0:T(4,128)S(1)} %get-tuple-element.49) | copy-start | bytes 196612
  2.5 4.1 %copy-start.8 = (f32[1,16,4,256]{3,2,1,0:T(4,128)}, f32[1,16,4,256]{3,2,1,0:T(4,128)S(1)}, u32[]{:S(2)}) copy-start(f32[1,16,4,256]{3,2,1,0:T(4,128)S(1)} %get-tuple-element.48) | copy-start | bytes 196612
  2.5 4.2 %copy-start.6 = (f32[1,16,4,256]{3,2,1,0:T(4,128)}, f32[1,16,4,256]{3,2,1,0:T(4,128)S(1)}, u32[]{:S(2)}) copy-start(f32[1,16,4,256]{3,2,1,0:T(4,128)S(1)} %get-tuple-element.47) | copy-start | bytes 196612
  2.5 4.2 %copy-start.4 = (f32[1,16,4,256]{3,2,1,0:T(4,128)}, f32[1,16,4,256]{3,2,1,0:T(4,128)S(1)}, u32[]{:S(2)}) copy-start(f32[1,16,4,256]{3,2,1,0:T(4,128)S(1)} %get-tuple-element.46) | copy-start | bytes 196612
  2.5 4.4 %copy-start.2 = (f32[1,16,4,256]{3,2,1,0:T(4,128)}, f32[1,16,4,256]{3,2,1,0:T(4,128)S(1)}, u32[]{:S(2)}) copy-start(f32[1,16,4,256]{3,2,1,0:T(4,128)S(1)} %get-tuple-element.45) | copy-start | bytes 196612
  2.5 4.4 %copy-start.30 = (f32[1,16,4,256]{3,2,1,0:T(4,128)}, f32[1,16,4,256]{3,2,1,0:T(4,128)S(1)}, u32[]{:S(2)}) copy-start(f32[1,16,4,256]{3,2,1,0:T(4,128)S(1)} %get-tuple-element.62) | copy-start | bytes 196612
  7.8 6.4 %collective-permute-start = (f32[20,16,4,1]{0,1,3,2:T(8,128)S(1)}, f32[20,16,4,1]{0,1,3,2:T(8,128)S(1)}, u32[]{:S(2)}, u32[]{:S(2)}) collective-permute-start(f32[20,16,4,1]{0,1,3,2:T(8,128)S(1)} %copy.224), channel_id=1, source_target_pairs={{0,8},{8,16},{16,24},{1,9},{9,17},{17,25},{2,10},{10,18},{18,26},{... | collective-permute-start | bytes 15368 | tf_op jit(solution)/shard_map/ppermute | solution.py:43
  11.8 5.8 %collective-permute-start.1 = (f32[20,16,4,1]{0,1,3,2:T(8,128)S(1)}, f32[20,16,4,1]{0,1,3,2:T(8,128)S(1)}, u32[]{:S(2)}, u32[]{:S(2)}) collective-permute-start(f32[20,16,4,1]{0,1,3,2:T(8,128)S(1)} %copy.226), channel_id=1, source_target_pairs={{8,0},{16,8},{24,16},{9,1},{17,9},{25,17},{10,2},{18,10},{26,18},{... | collective-permute-start | bytes 15368 | tf_op jit(solution)/shard_map/ppermute | solution.py:44
  18.4 6.0 %copy-start.1 = (f32[7,4,16,256]{3,2,1,0:T(8,128)S(1)}, f32[7,4,16,256]{3,2,1,0:T(8,128)}, u32[]{:S(2)}) copy-start(f32[7,4,16,256]{3,2,1,0:T(8,128)} %param.7) | copy-start | bytes 1376260
  18.4 12.7 %copy-start.39 = (s32[16,4,256]{2,1,0:T(4,128)S(1)}, s32[16,4,256]{2,1,0:T(4,128)}, u32[]{:S(2)}) copy-start(s32[16,4,256]{2,1,0:T(4,128)} %param.6) | copy-start | bytes 196612
  18.4 12.7 %copy-start.40 = (f32[16,4,256]{2,0,1:T(8,128)S(1)}, f32[16,4,256]{2,0,1:T(8,128)}, u32[]{:S(2)}) copy-start(f32[16,4,256]{2,0,1:T(8,128)} %get-tuple-element.34) | copy-start | bytes 196612
  18.8 12.6 %collective-permute-start.2 = (f32[20,16,1,258]{3,1,2,0:T(8,128)S(1)}, f32[20,16,1,258]{3,1,2,0:T(8,128)S(1)}, u32[]{:S(2)}, u32[]{:S(2)}) collective-permute-start(f32[20,16,1,258]{3,1,2,0:T(8,128)S(1)} %get-tuple-element.40), channel_id=1, source_target_pairs={{0,1},{1,2},{2,3},{3,4},{4,5},{5,6},{6,7},{8,9},{9,10},{10,11},{11... | collective-permute-start | bytes 990728 | tf_op jit(solution)/shard_map/ppermute | solution.py:43
  20.8 10.7 %collective-permute-start.3 = (f32[20,16,1,258]{3,1,2,0:T(8,128)S(1)}, f32[20,16,1,258]{3,1,2,0:T(8,128)S(1)}, u32[]{:S(2)}, u32[]{:S(2)}) collective-permute-start(f32[20,16,1,258]{3,1,2,0:T(8,128)S(1)} %get-tuple-element.41), channel_id=1, source_target_pairs={{1,0},{2,1},{3,2},{4,3},{5,4},{6,5},{7,6},{9,8},{10,9},{11,10},{12... | collective-permute-start | bytes 990728 | tf_op jit(solution)/shard_map/ppermute | solution.py:44
  25.2 18.6 %collective-permute-start.4 = (f32[7,4,16,1]{3,2,1,0:T(8,128)}, f32[7,4,16,1]{3,2,1,0:T(8,128)}, u32[]{:S(2)}, u32[]{:S(2)}) collective-permute-start(f32[7,4,16,1]{3,2,1,0:T(8,128)} %get-tuple-element.68), channel_id=1, source_target_pairs={{8,0},{16,8},{24,16},{9,1},{17,9},{25,17},{10,2},{18,10},{26,18},{... | collective-permute-start | bytes 5384 | tf_op jit(solution)/shard_map/ppermute | solution.py:44
  27.6 16.2 %collective-permute-start.5 = (f32[7,4,16,1]{3,2,1,0:T(8,128)}, f32[7,4,16,1]{3,2,1,0:T(8,128)}, u32[]{:S(2)}, u32[]{:S(2)}) collective-permute-start(f32[7,4,16,1]{3,2,1,0:T(8,128)} %get-tuple-element.67), channel_id=1, source_target_pairs={{0,8},{8,16},{16,24},{1,9},{9,17},{17,25},{2,10},{10,18},{18,26},{... | collective-permute-start | bytes 5384 | tf_op jit(solution)/shard_map/ppermute | solution.py:43
  38.1 23.6 %all-to-all-start = ((f32[4,16,4,256]{3,0,2,1:T(4,128)}), f32[4,16,4,256]{3,0,2,1:T(4,128)S(1)}, u32[]{:S(2)}, u32[]{:S(2)}) async-start(f32[4,16,4,256]{3,0,2,1:T(4,128)} %pad_maximum_fusion.3), calls=%async_computation | async-start | bytes 524288 | tf_op jit(solution)/shard_map/all_to_all | solution.py:107
  45.2 4.9 %collective-permute-start.6 = (f32[7,4,1,258]{3,2,1,0:T(1,128)S(1)}, f32[7,4,1,258]{3,2,1,0:T(1,128)S(1)}, u32[]{:S(2)}, u32[]{:S(2)}) collective-permute-start(f32[7,4,1,258]{3,2,1,0:T(1,128)S(1)} %get-tuple-element.66), channel_id=1, source_target_pairs={{4,0},{5,1},{6,2},{7,3},{12,8},{13,9},{14,10},{15,11},{20,16},{21,... | collective-permute-start | bytes 86696 | tf_op jit(solution)/shard_map/ppermute | solution.py:44
  48.4 5.9 %collective-permute-start.7 = (f32[7,4,1,258]{3,2,1,0:T(1,128)S(1)}, f32[7,4,1,258]{3,2,1,0:T(1,128)S(1)}, u32[]{:S(2)}, u32[]{:S(2)}) collective-permute-start(f32[7,4,1,258]{3,2,1,0:T(1,128)S(1)} %get-tuple-element.65), channel_id=1, source_target_pairs={{0,4},{1,5},{2,6},{3,7},{8,12},{9,13},{10,14},{11,15},{16,20},{17,... | collective-permute-start | bytes 86696 | tf_op jit(solution)/shard_map/ppermute | solution.py:43
  55.5 6.9 %collective-permute-start.8 = (f32[7,1,18,258]{3,2,1,0:T(8,128)S(1)}, f32[7,1,18,258]{3,2,1,0:T(8,128)S(1)}, u32[]{:S(2)}, u32[]{:S(2)}) collective-permute-start(f32[7,1,18,258]{3,2,1,0:T(8,128)S(1)} %get-tuple-element.64), channel_id=1, source_target_pairs={{1,0},{2,1},{3,2},{5,4},{6,5},{7,6},{9,8},{10,9},{11,10},{13,12},{... | collective-permute-start | bytes 390104 | tf_op jit(solution)/shard_map/ppermute | solution.py:44
  57.5 7.6 %collective-permute-start.9 = (f32[7,1,18,258]{3,2,1,0:T(8,128)S(1)}, f32[7,1,18,258]{3,2,1,0:T(8,128)S(1)}, u32[]{:S(2)}, u32[]{:S(2)}) collective-permute-start(f32[7,1,18,258]{3,2,1,0:T(8,128)S(1)} %get-tuple-element.63), channel_id=1, source_target_pairs={{0,1},{1,2},{2,3},{4,5},{5,6},{6,7},{8,9},{9,10},{10,11},{12,13},{... | collective-permute-start | bytes 390104 | tf_op jit(solution)/shard_map/ppermute | solution.py:43
  (23 other events, 41.3 us)
where the time goes:
time: 67.8 us; the launch traced here: 67.1 us
  starting transfers between devices  31.7 us (47%)
  other arithmetic  10.2 us (15%)
  waiting for transfers between devices  10.1 us (15%)
  local copies, waits for them, and re-layouts  9.56 us (14%)
  matrix products  3.62 us (5%)
  between operations  1.9 us (3%)
    ppermute x5, starting transfers between devices, padded_2(): after = lax.ppermute(leading, axis, down)  13.6 us
    ppermute x5, starting transfers between devices, padded_2(): before = lax.ppermute(last, axis, up)  12.5 us
    ppermute x5, waiting for transfers between devices, padded_2(): before = lax.ppermute(last, axis, up)  7.01 us
    all_to_all x1, starting transfers between devices, per_device(): lax.all_to_all(carried, 'gz', split_axis=1, concat_axis=2, tiled=True)  5.71 us
    concatenate x3, other arithmetic, padded_2(): value = jnp.concatenate([before, value, after], axis=dim)  4.26 us
    unnamed x107, local copies, waits for them, and re-layouts  3.96 us
    ppermute x5, waiting for transfers between devices, padded_2(): after = lax.ppermute(leading, axis, down)  3.12 us
    unnamed x25, other arithmetic  2.2 us
  transfers between devices with their start and end apart: 11, of which 4 were waited for; matrix products, arithmetic and copies ran while one was open for 20% of the time, Pallas kernels for 0%

commit v1 on v0

v1 whole, which is shorter than its diff:
```python
import functools

import jax
import jax.numpy as jnp
from jax import lax
from jax.experimental import pallas as pl
from jax.experimental.pallas import tpu as pltpu
from jax.sharding import PartitionSpec as P

VEL19 = [
    (0, 0, 0), (1, 0, 0), (-1, 0, 0), (0, 1, 0), (0, -1, 0), (0, 0, 1), (0, 0, -1),
    (1, 1, 0), (-1, -1, 0), (1, -1, 0), (-1, 1, 0), (1, 0, 1), (-1, 0, -1), (1, 0, -1),
    (-1, 0, 1), (0, 1, 1), (0, -1, -1), (0, 1, -1), (0, -1, 1),
]
WEIGHT19 = [1.0 / 3.0] + [1.0 / 18.0] * 6 + [1.0 / 36.0] * 12
OPPOSITE = [0, 2, 1, 4, 3, 6, 5, 8, 7, 10, 9, 12, 11, 14, 13, 16, 15, 18, 17]
OMEGA_FLOW = 1.6
OMEGA_FLUID = 1.25
OMEGA_SOLID = 1.6
BASE = 8
LANES = 128
MESH = pl.DeviceIdType.MESH

RIGHT = [1, 7, 9, 11, 13]
LEFT = [2, 8, 10, 12, 14]
UP = [7, 10, 3, 15, 17]
DOWN = [8, 9, 4, 16, 18]


def tree_sum(terms):
    terms = list(terms)
    while len(terms) > 1:
        terms = [sum(terms[i : i + 2][1:], terms[i]) for i in range(0, len(terms), 2)]
    return terms[0]


def momentum(pops):
    out = []
    for k in range(3):
        plus = tree_sum([pops[i] for i in range(19) if VEL19[i][k] > 0])
        minus = tree_sum([pops[i] for i in range(19) if VEL19[i][k] < 0])
        out.append(plus - minus)
    return out


def kernel(
    sizes, pops_hbm, cell_hbm, adj_hbm, flow_hbm, prev_hbm,
    pops, cells, adj, post, flags, prev,
    xs, xr, ys, yr, ds, tx, ty, tz, vel, vin, heat, hin,
    in_sem, out_sem, send_sem, recv_sem, tsend, trecv, vsend, vrecv, hsend, hrecv, vloc,
):
    ngx, ngy, ngz, depth, rows, cols = sizes
    layers = depth - BASE
    thick = depth // ngz
    solid_ranks = BASE // thick
    gx, gy, gz = lax.axis_index("gx"), lax.axis_index("gy"), lax.axis_index("gz")
    band = gy * ngz + gz
    nband = ngy * ngz

    def at(x, b):
        return {"gx": x, "gy": b // ngz, "gz": lax.rem(b, ngz)}

    has = {
        (1, 0): gx < ngx - 1, (-1, 0): gx > 0,
        (0, 1): band < nband - 1, (0, -1): band > 0,
    }
    for dx in (1, -1):
        for dy in (1, -1):
            has[dx, dy] = jnp.logical_and(has[dx, 0], has[0, dy])
    where_to = {key: at(gx + key[0], band + key[1]) for key in has}
    thermal_links = [
        (gx < ngx - 1, {"gx": gx + 1, "gy": gy, "gz": gz}),
        (gx > 0, {"gx": gx - 1, "gy": gy, "gz": gz}),
        (gy < ngy - 1, {"gx": gx, "gy": gy + 1, "gz": gz}),
        (gy > 0, {"gx": gx, "gy": gy - 1, "gz": gz}),
        (gz < ngz - 1, {"gx": gx, "gy": gy, "gz": gz + 1}),
        (gz > 0, {"gx": gx, "gy": gy, "gz": gz - 1}),
    ]
    peers = [{"gx": gx, "gy": gy, "gz": lax.rem(gz + k, ngz)} for k in range(1, ngz)]

    load_pops = pltpu.make_async_copy(pops_hbm.at[:, pl.ds(BASE, layers)], pops, in_sem.at[0])
    load_top = pltpu.make_async_copy(cell_hbm.at[pl.ds(BASE, 1)], cells.at[pl.ds(0, 1)], in_sem.at[1])
    load_low = pltpu.make_async_copy(cell_hbm.at[pl.ds(0, 1)], cells.at[pl.ds(1, 1)], in_sem.at[2])
    load_adj = pltpu.make_async_copy(adj_hbm, adj, in_sem.at[3])
    keep_low = pltpu.make_async_copy(
        pops_hbm.at[:, pl.ds(0, BASE)], flow_hbm.at[:, pl.ds(0, BASE)], out_sem.at[0]
    )
    load_pops.start()
    load_top.start()
    load_low.start()
    load_adj.start()
    keep_low.start()

    barrier = pltpu.get_barrier_semaphore()
    total = jnp.int32(ngz - 1)
    for peer in peers:
        pl.semaphore_signal(barrier, inc=1, device_id=peer, device_id_type=MESH)
    links = [(has[key], where_to[key]) for key in has] + thermal_links[2:4]
    for ok, target in links:
        @pl.when(ok)
        def _():
            pl.semaphore_signal(barrier, inc=1, device_id=target, device_id_type=MESH)
        total = total + ok.astype(jnp.int32)

    load_top.wait()
    load_low.wait()
    load_pops.wait()
    own_flag = jnp.where(cells[0] == 0, 1.0, 0.0)
    flags[0:rows, 0:cols] = own_flag
    heat[0] = cells[1].astype(jnp.float32)
    ys[0, layers] = own_flag[rows - 1 :]
    ys[1, layers] = own_flag[:1]
    lane = lax.broadcasted_iota(jnp.int32, (8, LANES), 1)

    def collide(l, carry):
        p = [pops[i, l] for i in range(19)]
        rho = tree_sum(p)
        m = momentum(p)
        inv = 1.0 / rho
        base = rho - 1.5 * (m[0] * m[0] + m[1] * m[1] + m[2] * m[2]) * inv
        inv45 = 4.5 * inv
        q = [None] * 19
        q[0] = (1.0 - OMEGA_FLOW) * p[0] + (OMEGA_FLOW * WEIGHT19[0]) * base
        for i in range(1, 19, 2):
            cm = tree_sum([m[k] if VEL19[i][k] > 0 else -m[k] for k in range(3) if VEL19[i][k]])
            even = base + inv45 * cm * cm
            odd = 3.0 * cm
            w = OMEGA_FLOW * WEIGHT19[i]
            q[i] = (1.0 - OMEGA_FLOW) * p[i] + w * (even + odd)
            q[i + 1] = (1.0 - OMEGA_FLOW) * p[i + 1] + w * (even - odd)
        for i in range(19):
            post[i, l + 1, 0:rows, 0:cols] = q[i]
        for side, (names, row) in enumerate(((UP, rows - 1), (DOWN, 0))):
            for k, i in enumerate(names):
                ys[side, l + k * layers + (1 if k else 0)] = q[i][row : row + 1]
        for side, names in enumerate((RIGHT, LEFT)):
            first = cols - LANES if side == 0 else 0
            edge = 1 if side == 0 else 0
            packed = jnp.zeros((8, LANES), jnp.float32)
            for k, i in enumerate(names):
                tile = post[i, l + 1, :, first : first + LANES]
                packed = jnp.where(lane == k, pltpu.roll(tile, (k + edge) % LANES, 1), packed)
            tile = flags[:, first : first + LANES]
            k = len(names)
            packed = jnp.where(lane == k, pltpu.roll(tile, (k + edge) % LANES, 1), packed)
            xs[side, l] = packed[0:rows]
        return carry

    lax.fori_loop(0, layers, collide, 0)

    pl.semaphore_wait(barrier, total)

    def remote(src, dst, ssem, rsem, target):
        return pltpu.make_async_remote_copy(
            src_ref=src, dst_ref=dst, send_sem=ssem, recv_sem=rsem,
            device_id=target, device_id_type=MESH,
        )

    last = pl.ds(cols - LANES, LANES)
    lead = pl.ds(0, LANES)
    jobs = [
        ((1, 0), xs.at[0], xr.at[0]),
        ((-1, 0), xs.at[1], xr.at[1]),
        ((0, 1), ys.at[0], yr.at[0]),
        ((0, -1), ys.at[1], yr.at[1]),
        ((1, 1), ys.at[0, pl.ds(0, layers + 1), :, last], ds.at[0]),
        ((-1, 1), ys.at[0, pl.ds(layers, layers + 1), :, lead], ds.at[1]),
        ((-1, -1), ys.at[1, pl.ds(0, layers + 1), :, lead], ds.at[2]),
        ((1, -1), ys.at[1, pl.ds(layers, layers + 1), :, last], ds.at[3]),
    ]
    flow_copies = []
    for n, (way, src, dst) in enumerate(jobs):
        copy = remote(src, dst, send_sem.at[n], recv_sem.at[n], where_to[way])
        flow_copies.append((copy, has[way], has[-way[0], -way[1]]))
    for copy, ok, _ in flow_copies:
        pl.when(ok)(copy.start)

    tcopies = []
    tjobs = [
        (1, adj_hbm.at[2, :, :, last], tx.at[1], 0),
        (0, adj_hbm.at[1, :, :, lead], tx.at[0], 1),
        (3, adj_hbm.at[4, :, pl.ds(adj.shape[2] - 8, 8), :], ty.at[1], 2),
        (2, adj_hbm.at[3, :, pl.ds(0, 8), :], ty.at[0], 3),
        (5, adj_hbm.at[6, thick - 1], tz.at[1], 4),
        (4, adj_hbm.at[5, 0], tz.at[0], 5),
    ]
    for sem, src, dst, link in tjobs:
        copy = remote(src, dst, tsend.at[sem], trecv.at[sem], thermal_links[link][1])
        tcopies.append((copy, thermal_links[link][0], thermal_links[link ^ 1][0], dst))
    for copy, ok, _, _ in tcopies:
        pl.when(ok)(copy.start)
    heat_send = remote(heat, hin.at[gz], hsend, hrecv.at[gz], {"gx": gx, "gy": gy, "gz": 0})
    pl.when(gz > 0)(heat_send.start)

    for n, (copy, _, ok) in enumerate(flow_copies):
        pl.when(ok)(copy.wait_recv)

        @pl.when(jnp.logical_not(ok))
        def _():
            if n < 2:
                xr[n, 0] = jnp.zeros((rows, LANES), jnp.float32)
            elif n < 4:
                yr[n - 2, layers] = jnp.zeros((1, cols), jnp.float32)
            else:
                ds[n - 4, layers if n % 2 == 0 else 0] = jnp.zeros((1, LANES), jnp.float32)

    kf = len(RIGHT)

    def pad8(v):
        return jnp.concatenate([v, jnp.zeros((8 - rows, LANES), jnp.float32)], axis=0)

    def halo_in(l, carry):
        for side, names in enumerate((RIGHT, LEFT)):
            packed = pad8(xr[side, l])
            for k, i in enumerate(names):
                shift = (127 - k) if side == 0 else (LANES - k) % LANES
                post[i, l + 1, 0:rows, cols : cols + LANES] = pltpu.roll(packed, shift, 1)[0:rows]
        for side, names in enumerate((UP, DOWN)):
            row = 7 if side == 0 else rows
            for k, i in enumerate(names):
                post[i, l + 1, row : row + 1, 0:cols] = yr[side, l + k * layers + (1 if k else 0)]
        for n, (i, row, off) in enumerate(((7, 7, 0), (10, 7, 1), (8, rows, 0), (9, rows, 1))):
            post[i, l + 1, row : row + 1, cols : cols + LANES] = ds[n, l + off]
        return carry

    lax.fori_loop(0, layers, halo_in, 0)
    from_left = pltpu.roll(pad8(xr[0, 0]), 127 - kf, 1)
    from_right = pltpu.roll(pad8(xr[1, 0]), LANES - kf, 1)
    flags[0:rows, cols:] = jnp.where(lane < 64, from_right, from_left)[0:rows]
    flags[7:8, 0:cols] = yr[0, layers]
    flags[rows : rows + 1, 0:cols] = yr[1, layers]
    flags[7:8, cols:] = jnp.where(lane[:1] < 64, ds[1, 0], ds[0, layers])
    flags[rows : rows + 1, cols:] = jnp.where(lane[:1] < 64, ds[2, layers], ds[3, 0])

    wide = cols + LANES

    def shifted(v, cx, cy):
        if cy:
            v = pltpu.roll(v, 1 if cy > 0 else 7, 0)
        if cx:
            v = pltpu.roll(v, 1 if cx > 0 else wide - 1, 1)
        return v[0:rows, 0:cols]

    flag_all = flags[...]
    pulled_flag = {
        (cx, cy): shifted(flag_all, cx, cy) for cx in (-1, 0, 1) for cy in (-1, 0, 1)
        if cx == 0 or cy == 0 or True
    }
    me = own_flag > 0.5
    for cut in range(ngz - solid_ranks):
        vel[cut, 3 * thick] = own_flag

    def stream(l, cut, inner):
        out = []
        for i in range(19):
            cx, cy, cz = VEL19[i]
            span = wide if cx else cols
            src = shifted_span(post[i, l + 1 - cz, :, 0:span], cx, cy)
            flag = pulled_flag[cx, cy]
            if cz > 0:
                flag = jnp.where(l > 0, flag, 0.0)
            if cz < 0:
                flag = jnp.where(l < layers - 1, flag, 0.0)
            back = post[OPPOSITE[i], l + 1, 0:rows, 0:cols]
            got = jnp.where(flag > 0.5, src, back)
            out.append(jnp.where(me, got, pops[i, l]))
        for i in range(19):
            pops[i, l] = out[i]
        scale = own_flag / tree_sum(out)
        m = momentum(out)
        for k in range(3):
            vel[cut, k * thick + inner] = m[k] * scale

    def shifted_span(v, cx, cy):
        if cy:
            v = pltpu.roll(v, 1 if cy > 0 else 7, 0)
        if cx:
            v = pltpu.roll(v, 1 if cx > 0 else wide - 1, 1)
        return v[0:rows, 0:cols]

    vel_copies = []
    for cut in range(ngz - solid_ranks):
        def step(inner, carry, cut=cut):
            stream(cut * thick + inner, cut, inner)
            return carry

        lax.fori_loop(0, thick, step, 0)
        to = cut + solid_ranks
        copy = remote(
            vel.at[cut], vin.at[gz], vsend.at[cut], vrecv.at[gz], {"gx": gx, "gy": gy, "gz": to}
        )
        local = pltpu.make_async_copy(vel.at[cut], vin.at[gz], vloc)
        pl.when(gz != to)(copy.start)
        pl.when(gz == to)(local.start)
        vel_copies.append((copy, local, to))

    store_flow = pltpu.make_async_copy(
        pops, flow_hbm.at[:, pl.ds(BASE, layers)], out_sem.at[1]
    )
    store_flow.start()

    load_adj.wait()
    for copy, _, ok, dst in tcopies:
        pl.when(ok)(copy.wait_recv)

        @pl.when(jnp.logical_not(ok))
        def _():
            dst[...] = jnp.zeros(dst.shape, jnp.float32)

    tall = adj.shape[2]

    def pulled_at(t):
        v = [adj[0, t]]
        v.append(pltpu.roll(jnp.concatenate([adj[1, t], tx[0, t]], 1), wide - 1, 1)[:, 0:cols])
        v.append(pltpu.roll(jnp.concatenate([adj[2, t], tx[1, t]], 1), 1, 1)[:, 0:cols])
        v.append(pltpu.roll(jnp.concatenate([adj[3, t], ty[0, t]], 0), tall + 7, 0)[0:tall])
        v.append(pltpu.roll(jnp.concatenate([adj[4, t], ty[1, t]], 0), 1, 0)[0:tall])
        v.append(adj[5, t + 1] if t + 1 < thick else tz[0])
        v.append(adj[6, t - 1] if t > 0 else tz[1])
        return v

    def mean_of(v):
        return 0.25 * v[0] + 0.125 * tree_sum(v[1:])

    @pl.when(gz < solid_ranks)
    def _():
        @pl.when(gz == 0)
        def _():
            for other in range(1, ngz):
                remote(heat, hin.at[other], hsend, hrecv.at[other], peers[0]).wait_recv()
            hin[0] = heat[...]
        for t in range(thick):
            v = pulled_at(t)
            core = OMEGA_SOLID * mean_of(v)
            if t == 0:
                codes = jnp.concatenate([hin[g, 0] for g in range(ngz)], axis=0)
                hot = jnp.where(codes == 2.0, 1.0, 0.0)
                core = core + jnp.where(gz == 0, hot, 0.0)
            for j in range(7):
                prev[j, t] = (1.0 - OMEGA_SOLID) * v[j] + core

    @pl.when(gz >= solid_ranks)
    def _():
        for source in range(ngz):
            @pl.when(gz != source)
            def _():
                remote(vel.at[0], vin.at[source], vsend.at[0], vrecv.at[source], peers[0]).wait_recv()
        pltpu.make_async_copy(vel.at[0], vin.at[gz], vloc).wait()
        wet = jnp.concatenate([vin[g, 3 * thick] for g in range(ngz)], axis=0)
        omega = jnp.where(wet > 0.5, OMEGA_FLUID, OMEGA_SOLID)
        rest = 1.0 - omega
        for t in range(thick):
            v = pulled_at(t)
            u = [
                jnp.concatenate([vin[g, k * thick + t] for g in range(ngz)], axis=0)
                for k in range(3)
            ]
            carried = (
                u[0] * (v[1] - v[2]) + u[1] * (v[3] - v[4]) + u[2] * (v[5] - v[6])
            )
            core = omega * (mean_of(v) + 0.5 * carried)
            for j in range(7):
                prev[j, t] = rest * v[j] + core

    store_prev = pltpu.make_async_copy(prev, prev_hbm, out_sem.at[2])
    store_prev.start()

    for copy, ok, _ in flow_copies:
        pl.when(ok)(copy.wait_send)
    for copy, ok, _, _ in tcopies:
        pl.when(ok)(copy.wait_send)
    pl.when(gz > 0)(heat_send.wait_send)
    for copy, _, to in vel_copies:
        pl.when(gz != to)(copy.wait_send)
    keep_low.wait()
    store_flow.wait()
    store_prev.wait()


def per_device(sizes, populations, cell_type, adjoint):
    ngx, ngy, ngz = sizes
    depth, rows, cols = cell_type.shape
    layers = depth - BASE
    thick, tall = adjoint.shape[1:3]
    nsend = ngz - BASE // thick
    f32 = jnp.float32
    nrow = 5 * layers + 1
    vm = lambda *shape: pltpu.VMEM(shape, f32)
    dma = lambda *shape: pltpu.SemaphoreType.DMA(shape)
    return pl.pallas_call(
        functools.partial(kernel, (ngx, ngy, ngz, depth, rows, cols)),
        out_shape=(
            jax.ShapeDtypeStruct(populations.shape, f32),
            jax.ShapeDtypeStruct(adjoint.shape, f32),
        ),
        in_specs=[pl.BlockSpec(memory_space=pl.ANY)] * 3,
        out_specs=(pl.BlockSpec(memory_space=pl.ANY),) * 2,
        scratch_shapes=[
            vm(19, layers, rows, cols),
            pltpu.VMEM((2, rows, cols), jnp.int32),
            vm(*adjoint.shape),
            vm(19, layers + 2, 8, cols + LANES),
            vm(8, cols + LANES),
            vm(*adjoint.shape),
            vm(2, layers, rows, LANES),
            vm(2, layers, rows, LANES),
            vm(2, nrow, 1, cols),
            vm(2, nrow, 1, cols),
            vm(4, layers + 1, 1, LANES),
            vm(2, thick, tall, LANES),
            vm(2, thick, 8, cols),
            vm(2, tall, cols),
            vm(nsend, 3 * thick + 1, rows, cols),
            vm(ngz, 3 * thick + 1, rows, cols),
            vm(1, rows, cols),
            vm(ngz, 1, rows, cols),
            dma(4), dma(3), dma(8), dma(8), dma(6), dma(6),
            dma(nsend), dma(ngz), pltpu.SemaphoreType.DMA, dma(ngz), pltpu.SemaphoreType.DMA,
        ],
        compiler_params=pltpu.CompilerParams(
            collective_id=0, has_side_effects=True, vmem_limit_bytes=40 * 1024 * 1024
        ),
        name="flow_thermal",
    )(populations, cell_type, adjoint)


def solution(mesh):
    placed = (
        P(None, None, ("gy", "gz"), "gx"),
        P(None, ("gy", "gz"), "gx"),
        P(None, "gz", "gy", "gx"),
    )
    sizes = (mesh.shape["gx"], mesh.shape["gy"], mesh.shape["gz"])
    return jax.shard_map(
        functools.partial(per_device, sizes),
        mesh=mesh,
        in_specs=placed,
        out_specs=(P(None, None, ("gy", "gz"), "gx"), P(None, "gz", "gy", "gx")),
        check_vma=False,
    )
```

time: 67.8 us -> 18 us (0.27)
  the two profiles are of different devices: /device:TPU:14 before, /device:TPU:7 now
where the time goes in v1:
time: 18 us; the launch traced here: 17.8 us
  Pallas kernels  12.2 us (68%)
  local copies, waits for them, and re-layouts  4.95 us (28%)
  between operations  0.65 us (4%)
    pallas_call x1, Pallas kernels, per_device(): pl.pallas_call(functools.partial(kernel, (ngx, ngy, ngz, depth, rows, col...  12.2 us
    unnamed x8, local copies, waits for them, and re-layouts  4.95 us

profile of v1, /device:TPU:7, one launch (start us, length us, event | category | flops | bytes accessed | tf_op | source)
XLA Modules:
  0.0 17.8 jit_solution(17243688613405727220)
XLA Ops:
  0.6 0.0 copy-start
  0.6 1.3 %copy-done = f32[19,16,4,256]{3,2,1,0:T(4,128)S(1)} copy-done((f32[19,16,4,256]{3,2,1,0:T(4,128)S(1)}, f32[19,16,4,256]{3,2,1,0:T(4,128)}, u32[]{:S(2)}) %copy-start) | copy-done | bytes 1245208
  1.9 0.0 copy-start.1
  1.9 1.0 %copy-done.1 = f32[7,4,16,256]{3,2,1,0:T(8,128)S(1)} copy-done((f32[7,4,16,256]{3,2,1,0:T(8,128)S(1)}, f32[7,4,16,256]{3,2,1,0:T(8,128)}, u32[]{:S(2)}) %copy-start.1) | copy-done | bytes 458776
  2.9 0.0 copy-start.2
  2.9 0.8 %copy-done.2 = s32[16,4,256]{2,1,0:T(4,128)S(1)} copy-done((s32[16,4,256]{2,1,0:T(4,128)S(1)}, s32[16,4,256]{2,1,0:T(4,128)}, u32[]{:S(2)}) %copy-start.2) | copy-done | bytes 65560
  3.8 12.2 %flow_thermal.1 = (f32[19,16,4,256]{3,2,1,0:T(4,128)S(1)}, f32[7,4,16,256]{3,2,1,0:T(8,128)S(1)}) custom-call(f32[19,16,4,256]{3,2,1,0:T(4,128)S(1)} %copy-done, s32[16,4,256]{2,1,0:T(4,128)S(1)} %copy-done.2, f32[7,4,16,256]{3,2,1,0:T(8,128)S(1)} %copy-done.1), custom_call_target="tpu_custom_call" | custom-call | tf_op jit(solution)/shard_map/flow_thermal/pallas_call | solution.py:390
  16.0 1.0 %copy.7 = f32[19,16,4,256]{3,2,1,0:T(4,128)} copy(f32[19,16,4,256]{3,2,1,0:T(4,128)S(1)} %get-tuple-element.4) | data formatting | bytes 2490368
  17.0 0.8 %copy.8 = f32[7,4,16,256]{3,2,1,0:T(8,128)} copy(f32[7,4,16,256]{3,2,1,0:T(8,128)S(1)} %get-tuple-element.5) | data formatting | bytes 917504
Async XLA Ops:
  0.6 1.3 %copy-start = (f32[19,16,4,256]{3,2,1,0:T(4,128)S(1)}, f32[19,16,4,256]{3,2,1,0:T(4,128)}, u32[]{:S(2)}) copy-start(f32[19,16,4,256]{3,2,1,0:T(4,128)} %pops_hbm.1) | copy-start | bytes 3735556
  1.9 1.0 %copy-start.1 = (f32[7,4,16,256]{3,2,1,0:T(8,128)S(1)}, f32[7,4,16,256]{3,2,1,0:T(8,128)}, u32[]{:S(2)}) copy-start(f32[7,4,16,256]{3,2,1,0:T(8,128)} %adj_hbm.1) | copy-start | bytes 1376260
  2.9 0.8 %copy-start.2 = (s32[16,4,256]{2,1,0:T(4,128)S(1)}, s32[16,4,256]{2,1,0:T(4,128)}, u32[]{:S(2)}) copy-start(s32[16,4,256]{2,1,0:T(4,128)} %cell_hbm.1) | copy-start | bytes 196612

commit v2 on v1

--- a/solution.py
+++ b/solution.py
@@ -44,10 +44,9 @@
 
 
 def kernel(
-    sizes, pops_hbm, cell_hbm, adj_hbm, flow_hbm, prev_hbm,
-    pops, cells, adj, post, flags, prev,
-    xs, xr, ys, yr, ds, tx, ty, tz, vel, vin, heat, hin,
-    in_sem, out_sem, send_sem, recv_sem, tsend, trecv, vsend, vrecv, hsend, hrecv, vloc,
+    sizes, pops_hbm, cell_hbm, adj_hbm, flow, vin, hin, tx, ty, tz,
+    cells, post, flags, xs, xr, ys, yr, ds, vel, planes,
+    in_sem, send_sem, recv_sem, tsend, trecv, vsend, vrecv, hsend, hrecv,
 ):
     ngx, ngy, ngz, depth, rows, cols = sizes
     layers = depth - BASE
@@ -78,18 +77,16 @@
     ]
     peers = [{"gx": gx, "gy": gy, "gz": lax.rem(gz + k, ngz)} for k in range(1, ngz)]
 
-    load_pops = pltpu.make_async_copy(pops_hbm.at[:, pl.ds(BASE, layers)], pops, in_sem.at[0])
+    upper = pl.ds(BASE, layers)
+    lower = pl.ds(0, BASE)
+    load_pops = pltpu.make_async_copy(pops_hbm.at[:, upper], flow.at[:, upper], in_sem.at[0])
     load_top = pltpu.make_async_copy(cell_hbm.at[pl.ds(BASE, 1)], cells.at[pl.ds(0, 1)], in_sem.at[1])
     load_low = pltpu.make_async_copy(cell_hbm.at[pl.ds(0, 1)], cells.at[pl.ds(1, 1)], in_sem.at[2])
-    load_adj = pltpu.make_async_copy(adj_hbm, adj, in_sem.at[3])
-    keep_low = pltpu.make_async_copy(
-        pops_hbm.at[:, pl.ds(0, BASE)], flow_hbm.at[:, pl.ds(0, BASE)], out_sem.at[0]
-    )
-    load_pops.start()
+    load_rest = pltpu.make_async_copy(pops_hbm.at[:, lower], flow.at[:, lower], in_sem.at[3])
     load_top.start()
     load_low.start()
-    load_adj.start()
-    keep_low.start()
+    load_pops.start()
+    load_rest.start()
 
     barrier = pltpu.get_barrier_semaphore()
     total = jnp.int32(ngz - 1)
@@ -107,13 +104,14 @@
     load_pops.wait()
     own_flag = jnp.where(cells[0] == 0, 1.0, 0.0)
     flags[0:rows, 0:cols] = own_flag
-    heat[0] = cells[1].astype(jnp.float32)
+    planes[0] = cells[1].astype(jnp.float32)
+    planes[1] = cells[0].astype(jnp.float32)
     ys[0, layers] = own_flag[rows - 1 :]
     ys[1, layers] = own_flag[:1]
     lane = lax.broadcasted_iota(jnp.int32, (8, LANES), 1)
 
     def collide(l, carry):
-        p = [pops[i, l] for i in range(19)]
+        p = [flow[i, BASE + l] for i in range(19)]
         rho = tree_sum(p)
         m = momentum(p)
         inv = 1.0 / rho
@@ -179,7 +177,7 @@
     tjobs = [
         (1, adj_hbm.at[2, :, :, last], tx.at[1], 0),
         (0, adj_hbm.at[1, :, :, lead], tx.at[0], 1),
-        (3, adj_hbm.at[4, :, pl.ds(adj.shape[2] - 8, 8), :], ty.at[1], 2),
+        (3, adj_hbm.at[4, :, pl.ds(adj_hbm.shape[2] - 8, 8), :], ty.at[1], 2),
         (2, adj_hbm.at[3, :, pl.ds(0, 8), :], ty.at[0], 3),
         (5, adj_hbm.at[6, thick - 1], tz.at[1], 4),
         (4, adj_hbm.at[5, 0], tz.at[0], 5),
@@ -189,8 +187,19 @@
         tcopies.append((copy, thermal_links[link][0], thermal_links[link ^ 1][0], dst))
     for copy, ok, _, _ in tcopies:
         pl.when(ok)(copy.start)
-    heat_send = remote(heat, hin.at[gz], hsend, hrecv.at[gz], {"gx": gx, "gy": gy, "gz": 0})
-    pl.when(gz > 0)(heat_send.start)
+    code_ranks = [0] + list(range(solid_ranks, ngz))
+    code_copies = []
+    for n, to in enumerate(code_ranks):
+        copy = remote(
+            planes.at[min(n, 1)], hin.at[gz], hsend.at[n], hrecv.at[gz],
+            {"gx": gx, "gy": gy, "gz": to},
+        )
+        pl.when(gz != to)(copy.start)
+        code_copies.append((copy, to))
+
+        @pl.when(gz == to)
+        def _():
+            hin[gz] = planes[min(n, 1)]
 
     for n, (copy, _, ok) in enumerate(flow_copies):
         pl.when(ok)(copy.wait_recv)
@@ -247,10 +256,7 @@
         if cx == 0 or cy == 0 or True
     }
     me = own_flag > 0.5
-    for cut in range(ngz - solid_ranks):
-        vel[cut, 3 * thick] = own_flag
-
-    def stream(l, cut, inner):
+    def stream(l, slot, to):
         out = []
         for i in range(19):
             cx, cy, cz = VEL19[i]
@@ -263,13 +269,22 @@
                 flag = jnp.where(l < layers - 1, flag, 0.0)
             back = post[OPPOSITE[i], l + 1, 0:rows, 0:cols]
             got = jnp.where(flag > 0.5, src, back)
-            out.append(jnp.where(me, got, pops[i, l]))
+            out.append(jnp.where(me, got, flow[i, BASE + l]))
         for i in range(19):
-            pops[i, l] = out[i]
+            flow[i, BASE + l] = out[i]
         scale = own_flag / tree_sum(out)
         m = momentum(out)
         for k in range(3):
-            vel[cut, k * thick + inner] = m[k] * scale
+            vel[l, k] = m[k] * scale
+        copy = remote(
+            vel.at[l], vin.at[gz, slot], vsend.at[to - solid_ranks], vrecv.at[gz],
+            {"gx": gx, "gy": gy, "gz": to},
+        )
+        pl.when(gz != to)(copy.start)
+
+        @pl.when(gz == to)
+        def _():
+            vin[gz, slot] = vel[l]
 
     def shifted_span(v, cx, cy):
         if cy:
@@ -278,28 +293,14 @@
             v = pltpu.roll(v, 1 if cx > 0 else wide - 1, 1)
         return v[0:rows, 0:cols]
 
-    vel_copies = []
-    for cut in range(ngz - solid_ranks):
-        def step(inner, carry, cut=cut):
-            stream(cut * thick + inner, cut, inner)
+    for to in range(solid_ranks, ngz):
+        def step(inner, carry, to=to):
+            stream((to - solid_ranks) * thick + inner, inner, to)
             return carry
 
         lax.fori_loop(0, thick, step, 0)
-        to = cut + solid_ranks
-        copy = remote(
-            vel.at[cut], vin.at[gz], vsend.at[cut], vrecv.at[gz], {"gx": gx, "gy": gy, "gz": to}
-        )
-        local = pltpu.make_async_copy(vel.at[cut], vin.at[gz], vloc)
-        pl.when(gz != to)(copy.start)
-        pl.when(gz == to)(local.start)
-        vel_copies.append((copy, local, to))
-
-    store_flow = pltpu.make_async_copy(
-        pops, flow_hbm.at[:, pl.ds(BASE, layers)], out_sem.at[1]
-    )
-    store_flow.start()
-
-    load_adj.wait()
+
+    load_rest.wait()
     for copy, _, ok, dst in tcopies:
         pl.when(ok)(copy.wait_recv)
 
@@ -307,7 +308,40 @@
         def _():
             dst[...] = jnp.zeros(dst.shape, jnp.float32)
 
-    tall = adj.shape[2]
+    for source in range(ngz):
+        own = {"gx": gx, "gy": gy, "gz": lax.rem(gz + 1, ngz)}
+        codes = remote(planes.at[0], hin.at[source], hsend.at[0], hrecv.at[source], own)
+        moved = remote(
+            vel.at[pl.ds(0, thick)], vin.at[source], vsend.at[0], vrecv.at[source], own
+        )
+        active = jnp.logical_and(gz >= solid_ranks, gz != source)
+        pl.when(jnp.logical_or(active, jnp.logical_and(gz == 0, gz != source)))(codes.wait_recv)
+        pl.when(active)(moved.wait_recv)
+
+    for copy, ok, _ in flow_copies:
+        pl.when(ok)(copy.wait_send)
+    for copy, ok, _, _ in tcopies:
+        pl.when(ok)(copy.wait_send)
+    for copy, to in code_copies:
+        pl.when(gz != to)(copy.wait_send)
+    for to in range(solid_ranks, ngz):
+        first = (to - solid_ranks) * thick
+        sent = remote(
+            vel.at[pl.ds(first, thick)], vin.at[0], vsend.at[to - solid_ranks], vrecv.at[0],
+            {"gx": gx, "gy": gy, "gz": to},
+        )
+        pl.when(gz != to)(sent.wait_send)
+
+
+def thermal_kernel(
+    sizes, flow, adj, vin, hin, tx, ty, tz, flow_hbm, prev_hbm, prev, out_sem,
+):
+    ngz, solid_ranks = sizes
+    gz = lax.axis_index("gz")
+    thick, tall, cols = adj.shape[1:]
+    wide = cols + LANES
+    store_flow = pltpu.make_async_copy(flow, flow_hbm, out_sem.at[0])
+    store_flow.start()
 
     def pulled_at(t):
         v = [adj[0, t]]
@@ -322,57 +356,34 @@
     def mean_of(v):
         return 0.25 * v[0] + 0.125 * tree_sum(v[1:])
 
+    def gathered(pick):
+        return jnp.concatenate([pick(g) for g in range(ngz)], axis=0)
+
     @pl.when(gz < solid_ranks)
     def _():
-        @pl.when(gz == 0)
-        def _():
-            for other in range(1, ngz):
-                remote(heat, hin.at[other], hsend, hrecv.at[other], peers[0]).wait_recv()
-            hin[0] = heat[...]
         for t in range(thick):
             v = pulled_at(t)
             core = OMEGA_SOLID * mean_of(v)
             if t == 0:
-                codes = jnp.concatenate([hin[g, 0] for g in range(ngz)], axis=0)
-                hot = jnp.where(codes == 2.0, 1.0, 0.0)
+                hot = jnp.where(gathered(lambda g: hin[g]) == 2.0, 1.0, 0.0)
                 core = core + jnp.where(gz == 0, hot, 0.0)
             for j in range(7):
                 prev[j, t] = (1.0 - OMEGA_SOLID) * v[j] + core
 
     @pl.when(gz >= solid_ranks)
     def _():
-        for source in range(ngz):
-            @pl.when(gz != source)
-            def _():
-                remote(vel.at[0], vin.at[source], vsend.at[0], vrecv.at[source], peers[0]).wait_recv()
-        pltpu.make_async_copy(vel.at[0], vin.at[gz], vloc).wait()
-        wet = jnp.concatenate([vin[g, 3 * thick] for g in range(ngz)], axis=0)
-        omega = jnp.where(wet > 0.5, OMEGA_FLUID, OMEGA_SOLID)
+        omega = jnp.where(gathered(lambda g: hin[g]) == 0.0, OMEGA_FLUID, OMEGA_SOLID)
         rest = 1.0 - omega
         for t in range(thick):
             v = pulled_at(t)
-            u = [
-                jnp.concatenate([vin[g, k * thick + t] for g in range(ngz)], axis=0)
-                for k in range(3)
-            ]
-            carried = (
-                u[0] * (v[1] - v[2]) + u[1] * (v[3] - v[4]) + u[2] * (v[5] - v[6])
-            )
+            u = [gathered(lambda g: vin[g, t, k]) for k in range(3)]
+            carried = u[0] * (v[1] - v[2]) + u[1] * (v[3] - v[4]) + u[2] * (v[5] - v[6])
             core = omega * (mean_of(v) + 0.5 * carried)
             for j in range(7):
                 prev[j, t] = rest * v[j] + core
 
-    store_prev = pltpu.make_async_copy(prev, prev_hbm, out_sem.at[2])
+    store_prev = pltpu.make_async_copy(prev, prev_hbm, out_sem.at[1])
     store_prev.start()
-
-    for copy, ok, _ in flow_copies:
-        pl.when(ok)(copy.wait_send)
-    for copy, ok, _, _ in tcopies:
-        pl.when(ok)(copy.wait_send)
-    pl.when(gz > 0)(heat_send.wait_send)
-    for copy, _, to in vel_copies:
-        pl.when(gz != to)(copy.wait_send)
-    keep_low.wait()
     store_flow.wait()
     store_prev.wait()
 
@@ -387,41 +398,50 @@
     nrow = 5 * layers + 1
     vm = lambda *shape: pltpu.VMEM(shape, f32)
     dma = lambda *shape: pltpu.SemaphoreType.DMA(shape)
-    return pl.pallas_call(
+    held = lambda *shape: jax.ShapeDtypeStruct(shape, f32)
+    hbm = pl.BlockSpec(memory_space=pltpu.HBM)
+    vmem = pl.BlockSpec(memory_space=pltpu.VMEM)
+    parts = pl.pallas_call(
         functools.partial(kernel, (ngx, ngy, ngz, depth, rows, cols)),
         out_shape=(
-            jax.ShapeDtypeStruct(populations.shape, f32),
-            jax.ShapeDtypeStruct(adjoint.shape, f32),
+            held(*populations.shape),
+            held(ngz, thick, 3, rows, cols),
+            held(ngz, rows, cols),
+            held(2, thick, tall, LANES),
+            held(2, thick, 8, cols),
+            held(2, tall, cols),
         ),
-        in_specs=[pl.BlockSpec(memory_space=pl.ANY)] * 3,
-        out_specs=(pl.BlockSpec(memory_space=pl.ANY),) * 2,
+        in_specs=[hbm] * 3,
+        out_specs=(vmem,) * 6,
         scratch_shapes=[
-            vm(19, layers, rows, cols),
             pltpu.VMEM((2, rows, cols), jnp.int32),
-            vm(*adjoint.shape),
             vm(19, layers + 2, 8, cols + LANES),
             vm(8, cols + LANES),
-            vm(*adjoint.shape),
             vm(2, layers, rows, LANES),
             vm(2, layers, rows, LANES),
             vm(2, nrow, 1, cols),
             vm(2, nrow, 1, cols),
             vm(4, layers + 1, 1, LANES),
-            vm(2, thick, tall, LANES),
-            vm(2, thick, 8, cols),
-            vm(2, tall, cols),
-            vm(nsend, 3 * thick + 1, rows, cols),
-            vm(ngz, 3 * thick + 1, rows, cols),
-            vm(1, rows, cols),
-            vm(ngz, 1, rows, cols),
-            dma(4), dma(3), dma(8), dma(8), dma(6), dma(6),
-            dma(nsend), dma(ngz), pltpu.SemaphoreType.DMA, dma(ngz), pltpu.SemaphoreType.DMA,
+            vm(layers, 3, rows, cols),
+            vm(2, rows, cols),
+            dma(4), dma(8), dma(8), dma(6), dma(6),
+            dma(nsend), dma(ngz), dma(nsend + 1), dma(ngz),
         ],
         compiler_params=pltpu.CompilerParams(
-            collective_id=0, has_side_effects=True, vmem_limit_bytes=40 * 1024 * 1024
+            collective_id=0, has_side_effects=True, vmem_limit_bytes=24 * 1024 * 1024
         ),
-        name="flow_thermal",
-    )(populations, cell_type, adjoint)
+        name="flow_step",
+    )(*[pltpu.with_memory_space_constraint(x, pltpu.HBM) for x in (populations, cell_type, adjoint)])
+    flow, vin, hin, tx, ty, tz = parts
+    return pl.pallas_call(
+        functools.partial(thermal_kernel, (ngz, BASE // thick)),
+        out_shape=(held(*populations.shape), held(*adjoint.shape)),
+        in_specs=[vmem] * 7,
+        out_specs=(hbm, hbm),
+        scratch_shapes=[vm(*adjoint.shape), dma(2)],
+        compiler_params=pltpu.CompilerParams(vmem_limit_bytes=16 * 1024 * 1024),
+        name="thermal_step",
+    )(flow, adjoint, vin, hin, tx, ty, tz)
 
 
 def solution(mesh):

time: 18 us -> 13.3 us (0.74)
  the two profiles are of different devices: /device:TPU:7 before, /device:TPU:0 now
where the time goes in v2:
time: 13.3 us; the launch traced here: 13.2 us
  Pallas kernels  12.5 us (94%)
  between operations  0.65 us (5%)
    pallas_call x1, Pallas kernels, per_device(): pl.pallas_call(functools.partial(kernel, (ngx, ngy, ngz, depth, rows, col...  11.3 us
    pallas_call x1, Pallas kernels, per_device(): pl.pallas_call(functools.partial(thermal_kernel, (ngz, BASE // thick)), o...  1.2 us

profile of v2, /device:TPU:0, one launch (start us, length us, event | category | flops | bytes accessed | tf_op | source)
XLA Modules:
  0.0 13.2 jit_solution(14846475021451410167)
XLA Ops:
  0.6 0.0 copy-start
  0.6 11.3 %flow_step.1 = (f32[19,16,4,256]{3,2,1,0:T(4,128)S(1)}, f32[4,4,3,4,256]{4,3,2,1,0:T(4,128)S(1)}, f32[4,4,256]{2,1,0:T(4,128)S(1)}, f32[2,4,16,128]{3,2,1,0:T(8,...) custom-call(f32[19,16,4,256]{3,2,1,0:T(4,128)} %pops_hbm.1, s32[16,4,256]{2,1,0:T(4,128)} %cell_hbm.1, ...), custom_call_target="tpu_custom_call" | custom-call | tf_op jit(solution)/shard_map/flow_step/pallas_call | solution.py:404
  12.0 0.0 copy-done
  12.0 1.2 %thermal_step.1 = (f32[19,16,4,256]{3,2,1,0:T(4,128)}, f32[7,4,16,256]{3,2,1,0:T(8,128)}) custom-call(f32[19,16,4,256]{3,2,1,0:T(4,128)S(1)} %get-tuple-element.8.flow, f32[7,4,16,256]{3,2,1,0:T(8,128)S(1)} %copy-done, f32[4,4,3,4,256]{4,3,2,1,0:T(4,128)S(1)} %get-tuple-element.9.vin, f32[4,4,256]{2,1,0:T(4,128)S(1)} %get-tuple-element.10.hin, ...), custom_call_target="tpu_custom_call" | custom-call | tf_op jit(solution)/shard_map/thermal_step/pallas_call | solution.py:436
Async XLA Ops:
  0.6 11.3 %copy-start = (f32[7,4,16,256]{3,2,1,0:T(8,128)S(1)}, f32[7,4,16,256]{3,2,1,0:T(8,128)}, u32[]{:S(2)}) copy-start(f32[7,4,16,256]{3,2,1,0:T(8,128)} %adj.1) | copy-start | bytes 1376260

commit v3 on v2

--- a/solution.py
+++ b/solution.py
@@ -83,21 +83,21 @@
     load_top = pltpu.make_async_copy(cell_hbm.at[pl.ds(BASE, 1)], cells.at[pl.ds(0, 1)], in_sem.at[1])
     load_low = pltpu.make_async_copy(cell_hbm.at[pl.ds(0, 1)], cells.at[pl.ds(1, 1)], in_sem.at[2])
     load_rest = pltpu.make_async_copy(pops_hbm.at[:, lower], flow.at[:, lower], in_sem.at[3])
-    load_top.start()
-    load_low.start()
-    load_pops.start()
-    load_rest.start()
-
     barrier = pltpu.get_barrier_semaphore()
     total = jnp.int32(ngz - 1)
-    for peer in peers:
-        pl.semaphore_signal(barrier, inc=1, device_id=peer, device_id_type=MESH)
-    links = [(has[key], where_to[key]) for key in has] + thermal_links[2:4]
+    links = [(has[key], where_to[key]) for key in reversed(list(has))] + thermal_links[2:4]
     for ok, target in links:
         @pl.when(ok)
         def _():
             pl.semaphore_signal(barrier, inc=1, device_id=target, device_id_type=MESH)
         total = total + ok.astype(jnp.int32)
+    for peer in peers:
+        pl.semaphore_signal(barrier, inc=1, device_id=peer, device_id_type=MESH)
+
+    load_top.start()
+    load_low.start()
+    load_pops.start()
+    load_rest.start()
 
     load_top.wait()
     load_low.wait()
@@ -144,7 +144,7 @@
             xs[side, l] = packed[0:rows]
         return carry
 
-    lax.fori_loop(0, layers, collide, 0)
+    lax.fori_loop(0, layers, collide, 0, unroll=2)
 
     pl.semaphore_wait(barrier, total)
 
@@ -170,7 +170,8 @@
     for n, (way, src, dst) in enumerate(jobs):
         copy = remote(src, dst, send_sem.at[n], recv_sem.at[n], where_to[way])
         flow_copies.append((copy, has[way], has[-way[0], -way[1]]))
-    for copy, ok, _ in flow_copies:
+    for n in (4, 5, 6, 7, 2, 3, 0, 1):
+        copy, ok, _ = flow_copies[n]
         pl.when(ok)(copy.start)
 
     tcopies = []
@@ -201,7 +202,13 @@
         def _():
             hin[gz] = planes[min(n, 1)]
 
-    for n, (copy, _, ok) in enumerate(flow_copies):
+    kf = len(RIGHT)
+
+    def pad8(v):
+        return jnp.concatenate([v, jnp.zeros((8 - rows, LANES), jnp.float32)], axis=0)
+
+    def arrive(n):
+        copy, _, ok = flow_copies[n]
         pl.when(ok)(copy.wait_recv)
 
         @pl.when(jnp.logical_not(ok))
@@ -213,26 +220,29 @@
             else:
                 ds[n - 4, layers if n % 2 == 0 else 0] = jnp.zeros((1, LANES), jnp.float32)
 
-    kf = len(RIGHT)
-
-    def pad8(v):
-        return jnp.concatenate([v, jnp.zeros((8 - rows, LANES), jnp.float32)], axis=0)
-
-    def halo_in(l, carry):
-        for side, names in enumerate((RIGHT, LEFT)):
+    for side, names in enumerate((RIGHT, LEFT)):
+        arrive(side)
+        def columns(l, carry, side=side, names=names):
             packed = pad8(xr[side, l])
             for k, i in enumerate(names):
                 shift = (127 - k) if side == 0 else (LANES - k) % LANES
                 post[i, l + 1, 0:rows, cols : cols + LANES] = pltpu.roll(packed, shift, 1)[0:rows]
-        for side, names in enumerate((UP, DOWN)):
-            row = 7 if side == 0 else rows
+            return carry
+
+        lax.fori_loop(0, layers, columns, 0, unroll=2)
+    for side, names in enumerate((UP, DOWN)):
+        arrive(2 + side)
+        row = 7 if side == 0 else rows
+        def edge_rows(l, carry, side=side, names=names, row=row):
             for k, i in enumerate(names):
                 post[i, l + 1, row : row + 1, 0:cols] = yr[side, l + k * layers + (1 if k else 0)]
-        for n, (i, row, off) in enumerate(((7, 7, 0), (10, 7, 1), (8, rows, 0), (9, rows, 1))):
+            return carry
+
+        lax.fori_loop(0, layers, edge_rows, 0, unroll=2)
+    for n, (i, row, off) in enumerate(((7, 7, 0), (10, 7, 1), (8, rows, 0), (9, rows, 1))):
+        arrive(4 + n)
+        for l in range(layers):
             post[i, l + 1, row : row + 1, cols : cols + LANES] = ds[n, l + off]
-        return carry
-
-    lax.fori_loop(0, layers, halo_in, 0)
     from_left = pltpu.roll(pad8(xr[0, 0]), 127 - kf, 1)
     from_right = pltpu.roll(pad8(xr[1, 0]), LANES - kf, 1)
     flags[0:rows, cols:] = jnp.where(lane < 64, from_right, from_left)[0:rows]
@@ -334,14 +344,18 @@
 
 
 def thermal_kernel(
-    sizes, flow, adj, vin, hin, tx, ty, tz, flow_hbm, prev_hbm, prev, out_sem,
+    sizes, flow, adj, vin, hin, tx, ty, tz, flow_hbm, prev_hbm, prev, flow_sem, prev_sem,
 ):
     ngz, solid_ranks = sizes
     gz = lax.axis_index("gz")
     thick, tall, cols = adj.shape[1:]
     wide = cols + LANES
-    store_flow = pltpu.make_async_copy(flow, flow_hbm, out_sem.at[0])
+    store_flow = pltpu.make_async_copy(flow, flow_hbm, flow_sem)
     store_flow.start()
+    stores = [
+        pltpu.make_async_copy(prev.at[:, t], prev_hbm.at[:, t], prev_sem.at[t])
+        for t in range(thick)
+    ]
 
     def pulled_at(t):
         v = [adj[0, t]]
@@ -369,6 +383,7 @@
                 core = core + jnp.where(gz == 0, hot, 0.0)
             for j in range(7):
                 prev[j, t] = (1.0 - OMEGA_SOLID) * v[j] + core
+            stores[t].start()
 
     @pl.when(gz >= solid_ranks)
     def _():
@@ -381,11 +396,11 @@
             core = omega * (mean_of(v) + 0.5 * carried)
             for j in range(7):
                 prev[j, t] = rest * v[j] + core
-
-    store_prev = pltpu.make_async_copy(prev, prev_hbm, out_sem.at[1])
-    store_prev.start()
+            stores[t].start()
+
+    for store in stores:
+        store.wait()
     store_flow.wait()
-    store_prev.wait()
 
 
 def per_device(sizes, populations, cell_type, adjoint):
@@ -438,7 +453,7 @@
         out_shape=(held(*populations.shape), held(*adjoint.shape)),
         in_specs=[vmem] * 7,
         out_specs=(hbm, hbm),
-        scratch_shapes=[vm(*adjoint.shape), dma(2)],
+        scratch_shapes=[vm(*adjoint.shape), pltpu.SemaphoreType.DMA, dma(thick)],
         compiler_params=pltpu.CompilerParams(vmem_limit_bytes=16 * 1024 * 1024),
         name="thermal_step",
     )(flow, adjoint, vin, hin, tx, ty, tz)

time: 13.3 us -> 12.8 us (0.962)
  Pallas kernels: 12.5 us -> 12 us
    pallas_call x1, Pallas kernels: 11.3 us -> 10.7 us  [per_device(): pl.pallas_call(functools.partial(kernel, (ngx, ngy, ngz, depth, rows, col...]
where the time goes in v3:
time: 12.8 us; the launch traced here: 12.6 us
  Pallas kernels  12 us (94%)
  between operations  0.65 us (5%)
    pallas_call x1, Pallas kernels, per_device(): pl.pallas_call(functools.partial(kernel, (ngx, ngy, ngz, depth, rows, col...  10.7 us
    pallas_call x1, Pallas kernels, per_device(): pl.pallas_call(functools.partial(thermal_kernel, (ngz, BASE // thick)), o...  1.22 us

profile of v3, /device:TPU:0, one launch (start us, length us, event | category | flops | bytes accessed | tf_op | source)
XLA Modules:
  0.0 12.6 jit_solution(8468825622360694422)
XLA Ops:
  0.6 0.0 copy-start
  0.6 10.7 %flow_step.1 = (f32[19,16,4,256]{3,2,1,0:T(4,128)S(1)}, f32[4,4,3,4,256]{4,3,2,1,0:T(4,128)S(1)}, f32[4,4,256]{2,1,0:T(4,128)S(1)}, f32[2,4,16,128]{3,2,1,0:T(8,...) custom-call(f32[19,16,4,256]{3,2,1,0:T(4,128)} %pops_hbm.1, s32[16,4,256]{2,1,0:T(4,128)} %cell_hbm.1, ...), custom_call_target="tpu_custom_call" | custom-call | tf_op jit(solution)/shard_map/flow_step/pallas_call | solution.py:419
  11.4 0.0 copy-done
  11.4 1.2 %thermal_step.1 = (f32[19,16,4,256]{3,2,1,0:T(4,128)}, f32[7,4,16,256]{3,2,1,0:T(8,128)}) custom-call(f32[19,16,4,256]{3,2,1,0:T(4,128)S(1)} %get-tuple-element.8.flow, f32[7,4,16,256]{3,2,1,0:T(8,128)S(1)} %copy-done, f32[4,4,3,4,256]{4,3,2,1,0:T(4,128)S(1)} %get-tuple-element.9.vin, f32[4,4,256]{2,1,0:T(4,128)S(1)} %get-tuple-element.10.hin, ...), custom_call_target="tpu_custom_call" | custom-call | tf_op jit(solution)/shard_map/thermal_step/pallas_call | solution.py:451
Async XLA Ops:
  0.6 10.8 %copy-start = (f32[7,4,16,256]{3,2,1,0:T(8,128)S(1)}, f32[7,4,16,256]{3,2,1,0:T(8,128)}, u32[]{:S(2)}) copy-start(f32[7,4,16,256]{3,2,1,0:T(8,128)} %adj.1) | copy-start | bytes 1376260
